TPU v7x, 32 devices: a whole 2x2x4 slice. The times are simulated.
32 devices in a mesh: panel: 16 (over z, y, core), rep: 2 (over x).
Axes of the slice: x: 2, y: 2, z: 4, core: 2. Of those that a mesh axis runs over, the one named last changes fastest.
Arguments:
- x_src: bfloat16 [2048, 128], P('panel'), may hold values from -6 to 6
- x_dst: bfloat16 [16384, 128], P(('panel', 'rep')), may hold values from -6 to 6
- weight: bfloat16 [128, 512], replicated, may hold values from -0.5 to 0.5
- att_src: float32 [8, 64], replicated, may hold values from -0.75 to 0.75
- att_dst: float32 [8, 64], replicated, may hold values from -0.75 to 0.75
- grad_out: bfloat16 [16384, 512], P(('panel', 'rep')), may hold values from -6 to 6
- block_rows: int32 [512], P(('panel', 'rep')), may hold values from 0 to 3, as said below
- block_cols: int32 [512], P(('panel', 'rep')), may hold values from 0 to 15
- block_masks: int32 [512, 128, 128], P(('panel', 'rep')), may hold values from 0 to 1, as said below
- block_counts: int32 [32], P(('panel', 'rep')), may hold values from 2 to 16, as said below
Outputs:
- grad_src: float32 [2048, 128], P('panel')
- grad_dst: float32 [16384, 128], P(('panel', 'rep'))
- grad_weight: float32 [128, 512], replicated
- grad_att_src: float32 [8, 64], replicated
- grad_att_dst: float32 [8, 64], replicated
Inputs may be any that keep to these rules, and one draw needn't show every extreme that they name: `block_counts`: live block slots of one device; at least one device has exactly 16. The pairs of block_rows and block_cols within one device's 16 slots are distinct. `block_masks`: slots at or after a device's count of live blocks hold only zeros.
All inputs are finite; a program needn't handle non-finite values.
Results may differ from a plain program's by a relative error of at most 0.012.
The roundings to bfloat16 on the way count: a program that leaves them out, or rounds other values in their place, can miss the bound.
Values may be sent and summed in bfloat16 or wider, within the bound.
A program may use at most 128 MiB of HBM per device.

v0:
```python
import jax
import jax.numpy as jnp
from jax import lax
from jax.experimental import pallas as pl
from jax.experimental.pallas import tpu as pltpu
from jax.sharding import PartitionSpec as P

F32 = jnp.float32
BF16 = jnp.bfloat16
MESH = pl.DeviceIdType.MESH
LANES = 128
CHUNK = 16
LOG2_E = 1.4426950408889634


def mm(a, b, ca=1, cb=0):
    return lax.dot_general(a, b, (((ca,), (cb,)), ((), ())), preferred_element_type=F32)


def split(values, parts):
    pieces = []
    for _ in range(parts):
        piece = values.astype(BF16)
        pieces.append(piece)
        values = values - piece.astype(F32)
    return pieces


def mm_split(a, b, parts, ca=1, cb=0):
    return sum(mm(piece, b, ca, cb) for piece in split(a, parts))


def edge_terms(pre):
    grown = 1.0 + jnp.exp2(-jnp.abs(pre))
    sigma = jnp.maximum(pre, 0.2 * pre) + 0.8 * jnp.log2(grown)
    return jnp.exp2(sigma), 0.6 + 0.4 * jnp.tanh((0.5 / LOG2_E) * pre)


def iota(shape, dim):
    return lax.broadcasted_iota(jnp.int32, shape, dim)


def layer_kernel(
    rows_ref, cols_ref, count_ref, x_all_ref, x_dst_ref, weight_ref, att_src_ref, att_dst_ref,
    grad_ref, masks_ref,
    grad_dst_ref, part_ref, part_att_ref,
    proj_src, proj_turned, proj_dst, cotan_turned, score_src, score_wide, inv_wide, weights, slopes,
    numer, denom, centre, grad_source, grad_score_src, grad_score_dst, source,
):
    heads, head_dim = att_src_ref.shape
    width = weight_ref.shape[1]
    pairs = width // LANES
    blk = masks_ref.shape[1]
    source_blocks = x_all_ref.shape[0] // blk
    dest = x_dst_ref.shape[0]
    count = count_ref[0]
    owners, share = part_ref.shape[1], part_ref.shape[2] - CHUNK
    reps = x_all_ref.shape[0] // source_blocks // share
    inputs = weight_ref.shape[0]

    lane_head = iota((heads, width), 1) // head_dim
    own = lane_head == iota((heads, width), 0)
    spread_src = jnp.where(own, jnp.concatenate([att_src_ref[...]] * heads, axis=1), 0.0)
    spread_dst = jnp.where(own, jnp.concatenate([att_dst_ref[...]] * heads, axis=1), 0.0)
    pad_rows = jnp.zeros((LANES - heads, width), F32)
    row = iota((LANES, width), 0)
    ones_heads = jnp.where(
        (lax.rem(row, heads) == iota((LANES, width), 1) // head_dim) & (row < 2 * heads), 1.0, 0.0
    ).astype(BF16)
    ones_turned = jnp.where(
        iota((width, LANES), 0) // head_dim == iota((width, LANES), 1), 1.0, 0.0
    ).astype(BF16)
    tall = jnp.concatenate([spread_src, spread_dst, pad_rows[heads:]], axis=0).astype(BF16)

    stack_src = jnp.concatenate([p.astype(F32) for p in split(spread_src, 3)], axis=0)
    stack_dst = jnp.concatenate([p.astype(F32) for p in split(spread_dst, 3)], axis=0)
    stacked = stack_src.astype(BF16)
    weight_turned = weight_ref[...].T
    proj_src[...] = mm(x_all_ref[...], weight_ref[...]).astype(BF16)
    per = min(4, source_blocks)
    for s in range(0, source_blocks, per):
        turned = mm(weight_turned, x_all_ref[s * blk : (s + per) * blk, :], 1, 1).astype(BF16)
        got = mm(stacked, turned)
        got = (got[:heads] + got[heads : 2 * heads] + got[2 * heads :]) * LOG2_E
        for n in range(per):
            proj_turned[s + n] = turned[:, n * blk : (n + 1) * blk]
            score_src[s + n] = got[:, n * blk : (n + 1) * blk]
    proj_dst[...] = mm(x_dst_ref[...], weight_ref[...]).astype(BF16)
    stacked = jnp.concatenate(
        [stack_dst, stack_src, jnp.zeros((LANES - 6 * heads, width), F32)], axis=0
    ).astype(BF16)
    got = mm(proj_dst[...], stacked, 1, 1) * LOG2_E
    shift = [got] + [pltpu.roll(got, LANES - n * heads, 1) for n in range(1, 6)]
    score_d = shift[0] + shift[1] + shift[2]
    pre_self = score_d + (shift[3] + shift[4] + shift[5])
    for h in range(heads):
        score_wide[h] = jnp.broadcast_to(score_d[:, h : h + 1], (dest, LANES))
    for d in range(dest // blk):
        cotan_turned[d] = grad_ref[d * blk : (d + 1) * blk, :].T

    numer[...] = jnp.zeros_like(numer)
    denom[...] = jnp.zeros_like(denom)
    grad_source[...] = jnp.zeros_like(grad_source)
    grad_score_src[...] = jnp.zeros_like(grad_score_src)
    grad_score_dst[...] = jnp.zeros_like(grad_score_dst)

    low = (iota((1, LANES), 1) < head_dim).astype(F32).astype(BF16)
    high = (iota((1, LANES), 1) >= head_dim).astype(F32).astype(BF16)
    second = iota((2 * blk, LANES), 0) // blk
    lane = iota((2 * blk, LANES), 1)

    def both(values):
        return jnp.concatenate([values * low, values * high], axis=0)

    ones_pair = [jnp.where(lane == 2 * g + second, 1.0, 0.0).astype(BF16) for g in range(pairs)]
    column = iota((LANES, 2 * blk), 0)
    column_head = iota((LANES, 2 * blk), 1) // blk
    minus_pair = [
        jnp.where(lax.rem(column, heads) == 2 * g + column_head, -1.0, 0.0) for g in range(pairs)
    ]
    minus_pair = [jnp.where(column < 2 * heads, m, 0.0).astype(BF16) for m in minus_pair]

    def forward(b, carry):
        r = pl.ds(pl.multiple_of(rows_ref[b] * blk, blk), blk)
        c = cols_ref[b]
        src = pl.ds(pl.multiple_of(c * blk, blk), blk)
        live = masks_ref[b] > 0
        scores = score_src[c]
        for g in range(pairs):
            at = slice(g * LANES, (g + 1) * LANES)
            found = []
            for h in (2 * g, 2 * g + 1):
                edge, slope = edge_terms(score_wide[h, r, :] + scores[h : h + 1, :])
                edge = jnp.where(live, edge, 0.0)
                weights[b, h] = edge
                slopes[b, h] = slope
                found.append(edge.astype(BF16))
            right = jnp.concatenate(
                [both(proj_src[src, at]), ones_pair[g]], axis=1
            )
            got = mm(jnp.concatenate(found, axis=1), right)
            numer[r, at] += got[:, :LANES]
            denom[r, :] += got[:, LANES:]
        return carry

    lax.fori_loop(0, count, forward, 0)

    lanes = iota((dest, LANES), 1)

    def two_pieces(values):
        top = values.astype(BF16).astype(F32)
        return (top + pltpu.roll(values - top, heads, 1)).astype(BF16)

    def over_heads(values):
        return jnp.where(lanes < heads, values, 0.0)

    feats = proj_dst[...].astype(F32)
    cotan = grad_ref[...].astype(F32)
    self_weight, self_slope = edge_terms(pre_self)
    self_weight = over_heads(self_weight)
    inverse = 1.0 / (denom[...] + jnp.where(lanes < heads, self_weight, 1.0))
    total = numer[...] + mm(two_pieces(self_weight), ones_heads) * feats
    attended = total * mm(two_pieces(over_heads(inverse)), ones_heads)
    narrow = over_heads(mm_split(cotan * attended, ones_turned, 2))
    centre[...] = two_pieces(narrow)
    self_att = self_weight * inverse
    self_pair = mm_split(cotan * feats, ones_turned, 2)
    self_grad = self_att * (self_pair - narrow) * self_slope
    for h in range(heads):
        inv_wide[h] = jnp.broadcast_to(inverse[:, h : h + 1], (dest, LANES))

    def backward(b, carry):
        d = rows_ref[b]
        r = pl.ds(pl.multiple_of(d * blk, blk), blk)
        c = cols_ref[b]
        nothing = jnp.zeros((head_dim, blk), BF16)
        for g in range(pairs):
            at = slice(g * LANES, (g + 1) * LANES)
            left = jnp.concatenate([grad_ref[r, at], centre[r, :]], axis=1)
            feats_turned = proj_turned[c, at, :]
            right = jnp.concatenate(
                [
                    jnp.concatenate([feats_turned[:head_dim], nothing], axis=1),
                    jnp.concatenate([nothing, feats_turned[head_dim:]], axis=1),
                    minus_pair[g],
                ],
                axis=0,
            )
            apart = mm(left, right)
            shares, sums = [], []
            for q in range(2):
                h = 2 * g + q
                share = weights[b, h] * inv_wide[h, r, :]
                grad = share * apart[:, q * blk : (q + 1) * blk] * slopes[b, h]
                sums.append(jnp.sum(grad, axis=0, keepdims=True))
                grad_score_dst[h, r, :] += grad
                shares.append(share.astype(BF16))
            grad_score_src[c, 2 * g : 2 * g + 2, :] += jnp.concatenate(sums, axis=0)
            got = mm(cotan_turned[d, at, :], jnp.concatenate(shares, axis=1))
            grad_source[c, at, :] += jnp.concatenate(
                [got[:head_dim, :blk], got[head_dim:, blk:]], axis=0
            )
        return carry

    lax.fori_loop(0, count, backward, 0)

    score_grad = self_grad
    for h in range(heads):
        score_grad += jnp.where(lanes == h, jnp.sum(grad_score_dst[h], axis=1, keepdims=True), 0.0)
    grads = (self_grad + pltpu.roll(score_grad, heads, 1)).astype(BF16)
    flat = (mm(two_pieces(self_att), ones_heads) * cotan + mm(grads, tall)).astype(BF16)
    grad_dst_ref[...] = mm(flat, weight_ref[...], 1, 1)
    part_weight = mm(x_dst_ref[...], flat, 0, 0)
    att_part = mm(grads, proj_dst[...], 0, 0)

    scores = jnp.concatenate([grad_score_src[s] for s in range(source_blocks)], axis=1).astype(BF16)
    spread_turned = spread_src.T.astype(BF16)
    for s in range(source_blocks):
        at = slice(s * blk, (s + 1) * blk)
        source[:, at] = (grad_source[s] + mm(spread_turned, scores[:, at])).astype(BF16)
    weight_turned_part = mm(source[...], x_all_ref[...])
    att_src_part = att_part[:heads] + mm(scores, proj_src[...])
    att_dst_part = att_part[heads : 2 * heads]
    for s in range(0, source_blocks, per):
        product = mm(weight_ref[...], source[:, s * blk : (s + per) * blk])
        for n in range(s, s + per):
            block = product[:, (n - s) * blk : (n - s + 1) * blk].T.astype(part_ref.dtype)
            for rep in range(reps):
                part_ref[n % 2, n // 2 * reps + rep, :share, :] = block[rep * share : (rep + 1) * share]
    part_weight += weight_turned_part.T
    tiles = [
        part_weight[n : n + CHUNK, g * LANES : (g + 1) * LANES].astype(part_ref.dtype)
        for g in range(pairs)
        for n in range(0, inputs, CHUNK)
    ]
    half = len(tiles) // 2
    for core in range(2):
        for owner in range(owners):
            part_ref[core, owner, share:, :] = (
                tiles[core * half + owner] if owner < half else jnp.zeros((CHUNK, LANES), part_ref.dtype)
            )
    src_row = jnp.sum(jnp.where(own, att_src_part, 0.0), axis=0, keepdims=True)
    dst_row = jnp.sum(jnp.where(own, att_dst_part, 0.0), axis=0, keepdims=True)
    stack = [row[:, g * LANES : (g + 1) * LANES] for row in (src_row, dst_row) for g in range(pairs)]
    att = jnp.concatenate(stack, axis=0)
    part_att_ref[...] = jnp.concatenate(
        [att.astype(BF16).astype(F32), att - att.astype(BF16).astype(F32)], axis=0
    ).astype(part_att_ref.dtype)


def place():
    panel, rep = lax.axis_index("panel"), lax.axis_index("rep")
    return panel // 2, panel % 2, rep, lax.axis_size("panel") // 2, lax.axis_size("rep")


def remote(src, dst, send, recv, panel, rep):
    return pltpu.make_async_remote_copy(
        src_ref=src, dst_ref=dst, send_sem=send, recv_sem=recv, device_id=(panel, rep), device_id_type=MESH
    )


def each(start, stop, step):
    def body(k, carry):
        step(k)
        return carry

    lax.fori_loop(start, stop, body, 0)


def gather_kernel(x_ref, out_ref, send, recv, pass_send, pass_recv):
    plane, core, rep, planes, _ = place()
    me = plane * 2 + core
    mate = plane * 2 + 1 - core
    barrier = pltpu.get_barrier_semaphore()

    def peer(k):
        return lax.rem(plane + k, planes) * 2 + core

    def greet(k):
        pl.semaphore_signal(barrier, inc=1, device_id=(peer(k), rep), device_id_type=MESH)

    each(1, planes, greet)
    pl.semaphore_signal(barrier, inc=1, device_id=(mate, rep), device_id_type=MESH)
    pl.semaphore_wait(barrier, planes)

    def own(k):
        return remote(x_ref, out_ref.at[me], send.at[k], recv.at[k], peer(k), rep)

    def passed(k):
        slot = lax.rem(plane + planes - k, planes) * 2 + core
        return remote(out_ref.at[slot], out_ref.at[slot], pass_send.at[k], pass_recv.at[k], mate, rep)

    each(1, planes, lambda k: own(k).start())
    first = remote(x_ref, out_ref.at[me], pass_send.at[0], pass_recv.at[0], mate, rep)
    first.start()
    out_ref[me] = x_ref[...]

    def hand_on(k):
        own(k).wait_recv()
        passed(k).start()

    each(1, planes, hand_on)
    first.wait()

    def finish(k):
        own(k).wait_send()
        passed(k).wait()

    each(1, planes, finish)


def gather(x_src):
    panels = lax.axis_size("panel")
    sems = pltpu.SemaphoreType.DMA((panels // 2,))
    vmem = pl.BlockSpec(memory_space=pltpu.VMEM)
    out = pl.pallas_call(
        gather_kernel,
        out_shape=jax.ShapeDtypeStruct((panels,) + x_src.shape, x_src.dtype),
        in_specs=[vmem],
        out_specs=vmem,
        scratch_shapes=[sems] * 4,
        compiler_params=pltpu.CompilerParams(collective_id=0, has_side_effects=True),
    )(x_src)
    return out.reshape(panels * x_src.shape[0], x_src.shape[1])


def reduce_kernel(
    part_ref, att_ref, grad_src_ref, grad_weight_ref, att_src_ref, att_dst_ref,
    mate_part, mate_att, merged, landed, chunks, chunk, mate_sems, send, recv, row_send, row_recv,
    chunk_send, chunk_recv,
):
    plane, core, rep, planes, reps = place()
    owners, rows = merged.shape[:2]
    share = rows - 2 * CHUNK
    devices = 2 * owners
    me = plane * reps + rep
    panel = plane * 2 + core
    mate = plane * 2 + 1 - core
    index = panel * reps + rep
    barrier = pltpu.get_barrier_semaphore()

    def other(k):
        e = lax.rem(index + k, devices)
        return e // reps, lax.rem(e, reps)

    def greet(k):
        pl.semaphore_signal(barrier, inc=1, device_id=other(k), device_id_type=MESH)

    each(1, devices, greet)
    pl.semaphore_wait(barrier, devices - 1)

    swap = remote(part_ref.at[1 - core], mate_part, mate_sems.at[0], mate_sems.at[1], mate, rep)
    swap_att = remote(att_ref, mate_att, mate_sems.at[2], mate_sems.at[3], mate, rep)
    swap.start()
    swap_att.start()
    swap_att.wait()
    pair_att = att_ref[...].astype(F32) + mate_att[...].astype(F32)
    pair_att = pair_att[: CHUNK // 2] + pair_att[CHUNK // 2 :]
    top = pair_att.astype(BF16).astype(F32)
    tail = jnp.concatenate([top, pair_att - top], axis=0).astype(BF16)
    swap.wait()

    def to_owner(k):
        d = lax.rem(me + k, owners)
        return remote(
            merged.at[d], landed.at[k], send.at[k], recv.at[k], d // reps * 2 + core, lax.rem(d, reps)
        )

    def merge(k):
        d = lax.rem(me + k, owners)
        summed = part_ref[core, d].astype(F32) + mate_part[d].astype(F32)
        merged[d, : share + CHUNK, :] = summed.astype(BF16)
        merged[d, share + CHUNK :, :] = tail

    def merge_send(k):
        merge(k)
        to_owner(k).start()

    each(1, owners, merge_send)
    merge(0)

    def collect(k, total):
        to_owner(k).wait_recv()
        return total + landed[k].astype(F32)

    total = lax.fori_loop(1, owners, collect, merged[me].astype(F32))

    chunk[...] = total[share : share + CHUNK].astype(BF16)

    def spread(k):
        e_panel, e_rep = other(k)
        return remote(chunk, chunks.at[index], chunk_send.at[k], chunk_recv.at[k], e_panel, e_rep)

    def rows_to(k):
        part = grad_src_ref.at[pl.ds(pl.multiple_of(rep * share, share), share)]
        return remote(part, part, row_send.at[k], row_recv.at[k], panel, lax.rem(rep + k, reps))

    grad_src_ref[pl.ds(pl.multiple_of(rep * share, share), share), :] = total[:share]
    each(1, devices, lambda k: spread(k).start())
    each(1, reps, lambda k: rows_to(k).start())
    chunks[index] = chunk[...]
    att = total[share + CHUNK :]
    att = att[: CHUNK // 2] + att[CHUNK // 2 :]
    heads, head_dim = att_src_ref.shape
    per = LANES // head_dim
    lines = [
        att[r : r + 1, q * head_dim : (q + 1) * head_dim] for r in range(2 * heads // per) for q in range(per)
    ]
    att_src_ref[...] = jnp.concatenate(lines[:heads], axis=0)
    att_dst_ref[...] = jnp.concatenate(lines[heads:], axis=0)
    each(1, owners, lambda k: to_owner(k).wait_send())
    each(1, devices, lambda k: spread(k).wait())
    each(1, reps, lambda k: rows_to(k).wait())
    inputs, width = grad_weight_ref.shape
    half = inputs * width // LANES // CHUNK // 2
    for n in range(2 * half):
        c, d = n // half, n % half
        sender = (d // reps * 2 + c) * reps + d % reps
        at, col = n * CHUNK % inputs, n * CHUNK // inputs * LANES
        grad_weight_ref[at : at + CHUNK, col : col + LANES] = chunks[sender].astype(F32)


def reduce(part, part_att, inputs, width, heads, rows):
    owners, lines = part.shape[1:3]
    reps = lax.axis_size("rep")
    vmem = pl.BlockSpec(memory_space=pltpu.VMEM)
    dma = pltpu.SemaphoreType.DMA
    return pl.pallas_call(
        reduce_kernel,
        out_shape=(
            jax.ShapeDtypeStruct((rows, inputs), F32),
            jax.ShapeDtypeStruct((inputs, width), F32),
            jax.ShapeDtypeStruct((heads, width // heads), F32),
            jax.ShapeDtypeStruct((heads, width // heads), F32),
        ),
        in_specs=[vmem] * 2,
        out_specs=(vmem,) * 4,
        scratch_shapes=[
            pltpu.VMEM((owners, lines, LANES), BF16),
            pltpu.VMEM((CHUNK, LANES), BF16),
            pltpu.VMEM((owners, lines + CHUNK, LANES), BF16),
            pltpu.VMEM((owners, lines + CHUNK, LANES), BF16),
            pltpu.VMEM((2 * owners, CHUNK, LANES), BF16),
            pltpu.VMEM((CHUNK, LANES), BF16),
            dma((4,)),
            dma((owners,)),
            dma((owners,)),
            dma((reps,)),
            dma((reps,)),
            dma((2 * owners,)),
            dma((2 * owners,)),
        ],
        compiler_params=pltpu.CompilerParams(
            collective_id=1, has_side_effects=True, vmem_limit_bytes=62 * 1024 * 1024
        ),
    )(part, part_att)


def layer(x_all, x_dst, weight, att_src, att_dst, grad_out, rows, cols, masks, counts):
    heads = att_src.shape[0]
    inputs, width = weight.shape
    slots, blk = masks.shape[:2]
    sources, dest = x_all.shape[0], x_dst.shape[0]
    blocks = sources // blk
    reps = lax.axis_size("rep")
    owners = blocks // 2 * reps
    vmem = pl.BlockSpec(memory_space=pltpu.VMEM)
    smem = pl.BlockSpec(memory_space=pltpu.SMEM)
    return pl.pallas_call(
        layer_kernel,
        out_shape=(
            jax.ShapeDtypeStruct((dest, inputs), F32),
            jax.ShapeDtypeStruct((2, owners, blk // reps + CHUNK, LANES), BF16),
            jax.ShapeDtypeStruct((CHUNK, LANES), BF16),
        ),
        in_specs=[smem] * 3 + [vmem] * 7,
        out_specs=(vmem,) * 3,
        scratch_shapes=[
            pltpu.VMEM((sources, width), BF16),
            pltpu.VMEM((blocks, width, blk), BF16),
            pltpu.VMEM((dest, width), BF16),
            pltpu.VMEM((dest // blk, width, blk), BF16),
            pltpu.VMEM((blocks, heads, blk), F32),
            pltpu.VMEM((heads, dest, LANES), F32),
            pltpu.VMEM((heads, dest, LANES), F32),
            pltpu.VMEM((slots, heads, blk, blk), F32),
            pltpu.VMEM((slots, heads, blk, blk), F32),
            pltpu.VMEM((dest, width), F32),
            pltpu.VMEM((dest, LANES), F32),
            pltpu.VMEM((dest, LANES), BF16),
            pltpu.VMEM((blocks, width, blk), F32),
            pltpu.VMEM((blocks, heads, blk), F32),
            pltpu.VMEM((heads, dest, LANES), F32),
            pltpu.VMEM((width, sources), BF16),
        ],
        compiler_params=pltpu.CompilerParams(vmem_limit_bytes=62 * 1024 * 1024),
    )(rows, cols, counts, x_all, x_dst, weight, att_src, att_dst, grad_out, masks)


def shards(
    x_src, x_dst, weight, att_src, att_dst, grad_out, block_rows, block_cols, block_masks, block_counts
):
    x_all = gather(x_src)
    grad_dst, part, part_att = layer(
        x_all, x_dst, weight, att_src, att_dst, grad_out, block_rows, block_cols, block_masks, block_counts
    )
    grad_src, grad_weight, grad_att_src, grad_att_dst = reduce(
        part, part_att, weight.shape[0], weight.shape[1], att_src.shape[0], x_src.shape[0]
    )
    return grad_src, grad_dst, grad_weight, grad_att_src, grad_att_dst


def solution(mesh):
    both = P(("panel", "rep"))
    return jax.shard_map(
        shards,
        mesh=mesh,
        in_specs=(P("panel", None), both, P(), P(), P(), both, both, both, both, both),
        out_specs=(P("panel", None), both, P(), P(), P()),
        check_vma=False,
    )
```

profile of v0, /device:TPU:0, one launch (start us, length us, event | category | flops | bytes accessed | tf_op | source)
XLA Modules:
  0.0 69.7 jit_solution(14654681935257900586)
XLA Ops:
  1.3 13.9 %shard_map.137 = bf16[16,128,128]{2,1,0:T(8,128)(2,1)} custom-call(bf16[128,128]{1,0:T(8,128)(2,1)} %x_ref.1), custom_call_target="tpu_custom_call" | custom-call | tf_op jit(solution)/shard_map/pallas_call | solution.py:316
  15.1 14.6 %shard_map.138 = (f32[512,128]{1,0:T(8,128)}, bf16[2,16,80,128]{3,2,1,0:T(8,128)(2,1)}, bf16[16,128]{1,0:T(8,128)(2,1)}) custom-call(s32[16]{0:T(128)} %rows_ref.1, s32[16]{0:T(128)} %cols_ref.1, s32[1]{0:T(128)S(6)} %copy.19.count_ref, bf16[2048,128]{1,0:T(8,128)(2,1)} %bitcast.1, bf16[512,128]{1,0:T(8,128)(2,1)} %x_dst_ref.1, bf16[128,512]{1,0:T(8,128)(2,1)} %weight_ref.1, ...), custom_call_target="tpu_custom_call" | custom-call | tf_op jit(solution)/shard_map/pallas_call | solution.py:469
  29.8 35.4 %shard_map.139 = (f32[128,128]{1,0:T(8,128)}, f32[128,512]{1,0:T(8,128)}, f32[8,64]{1,0:T(8,128)}, f32[8,64]{1,0:T(8,128)}) custom-call(bf16[2,16,80,128]{3,2,1,0:T(8,128)(2,1)} %get-tuple-element.12.part_ref, bf16[16,128]{1,0:T(8,128)(2,1)} %get-tuple-element.13.att_ref), custom_call_target="tpu_custom_call" | custom-call | tf_op jit(solution)/shard_map/pallas_call | solution.py:428
  65.2 1.5 %copy.20 = f32[128,128]{1,0:T(8,128)} copy(f32[128,128]{1,0:T(8,128)} %get-tuple-element.24) | data formatting | bytes 131072
  66.7 0.0 copy-start.1
  66.7 1.7 %copy.21 = f32[128,512]{1,0:T(8,128)} copy(f32[128,512]{1,0:T(8,128)} %get-tuple-element.26) | data formatting | bytes 524288
  68.4 0.0 copy-done.1
  68.4 0.0 copy-start
  68.4 0.6 copy.22
  69.0 0.1 copy-done
  69.1 0.6 copy.23
Async XLA Ops:
  66.7 1.7 %copy-start.1 = (f32[8,64]{1,0:T(8,128)S(1)}, f32[8,64]{1,0:T(8,128)}, u32[]{:S(2)}) copy-start(f32[8,64]{1,0:T(8,128)} %get-tuple-element.27) | copy-start | bytes 6148
  68.4 0.7 copy-start
where the time goes:
time: 69.2 us; the launch traced here: 69.7 us
  Pallas kernels  63.9 us (92%)
  local copies, waits for them, and re-layouts  4.42 us (6%)
  between operations  1.3 us (2%)
    pallas_call x1, Pallas kernels, reduce(): pl.pallas_call(reduce_kernel, out_shape=(jax.ShapeDtypeStruct((rows, inpu...  35.4 us
    pallas_call x1, Pallas kernels, layer(): pl.pallas_call(layer_kernel, out_shape=(jax.ShapeDtypeStruct((dest, input...  14.6 us
    pallas_call x1, Pallas kernels, gather(): pl.pallas_call(gather_kernel, out_shape=jax.ShapeDtypeStruct((panels,) +...  13.9 us
    unnamed x8, local copies, waits for them, and re-layouts  4.42 us

commit v1 on v0

--- a/solution.py
+++ b/solution.py
@@ -1,3 +1,5 @@
+import functools
+
 import jax
 import jax.numpy as jnp
 from jax import lax
@@ -325,13 +327,13 @@
 
 
 def reduce_kernel(
-    part_ref, att_ref, grad_src_ref, grad_weight_ref, att_src_ref, att_dst_ref,
-    mate_part, mate_att, merged, landed, chunks, chunk, mate_sems, send, recv, row_send, row_recv,
-    chunk_send, chunk_recv,
+    part_ref, att_ref, rows_ref, chunks, att_out_ref,
+    mate_part, mate_att, merged, landed, chunk, tail, att_landed, mate_sems, swap_send, swap_recv,
+    send, recv, row_send, row_recv, chunk_send, chunk_recv, att_send, att_recv, sum_send, sum_recv,
 ):
     plane, core, rep, planes, reps = place()
     owners, rows = merged.shape[:2]
-    share = rows - 2 * CHUNK
+    share = rows - CHUNK
     devices = 2 * owners
     me = plane * reps + rep
     panel = plane * 2 + core
@@ -349,57 +351,122 @@
     each(1, devices, greet)
     pl.semaphore_wait(barrier, devices - 1)
 
-    swap = remote(part_ref.at[1 - core], mate_part, mate_sems.at[0], mate_sems.at[1], mate, rep)
-    swap_att = remote(att_ref, mate_att, mate_sems.at[2], mate_sems.at[3], mate, rep)
-    swap.start()
+    pieces = swap_send.shape[0]
+    span = owners // pieces
+
+    def piece_at(n):
+        return lax.rem(me // span + 1 + n, pieces)
+
+    def swap(n):
+        n = piece_at(n)
+        piece = pl.ds(n * span, span)
+        return remote(
+            part_ref.at[1 - core, piece], mate_part.at[piece], swap_send.at[n], swap_recv.at[n], mate, rep
+        )
+
+    swap_att = remote(att_ref, mate_att, mate_sems.at[0], mate_sems.at[1], mate, rep)
+    each(0, pieces, lambda n: swap(n).start())
     swap_att.start()
+
+    def to_owner(d):
+        slot = lax.rem(me - d + owners, owners)
+        return remote(
+            merged.at[d], landed.at[slot], send.at[d], recv.at[slot], d // reps * 2 + core, lax.rem(d, reps)
+        )
+
+    def from_owner(k):
+        return remote(merged.at[0], landed.at[k], send.at[0], recv.at[k], mate, rep)
+
+    def merge_piece(n):
+        swap(n).wait_recv()
+
+        def merge_send(j):
+            d = piece_at(n) * span + lax.rem(me + j, span)
+            summed = part_ref[core, d].astype(F32) + mate_part[d].astype(F32)
+            merged[d] = summed.astype(BF16)
+
+            @pl.when(d != me)
+            def _():
+                to_owner(d).start()
+
+        each(0, span, merge_send)
+
+    each(0, pieces, merge_piece)
+
     swap_att.wait()
     pair_att = att_ref[...].astype(F32) + mate_att[...].astype(F32)
-    pair_att = pair_att[: CHUNK // 2] + pair_att[CHUNK // 2 :]
-    top = pair_att.astype(BF16).astype(F32)
-    tail = jnp.concatenate([top, pair_att - top], axis=0).astype(BF16)
-    swap.wait()
-
-    def to_owner(k):
-        d = lax.rem(me + k, owners)
-        return remote(
-            merged.at[d], landed.at[k], send.at[k], recv.at[k], d // reps * 2 + core, lax.rem(d, reps)
-        )
-
-    def merge(k):
-        d = lax.rem(me + k, owners)
-        summed = part_ref[core, d].astype(F32) + mate_part[d].astype(F32)
-        merged[d, : share + CHUNK, :] = summed.astype(BF16)
-        merged[d, share + CHUNK :, :] = tail
-
-    def merge_send(k):
-        merge(k)
-        to_owner(k).start()
-
-    each(1, owners, merge_send)
-    merge(0)
+
+    def as_pieces(pair):
+        folded = pair[: CHUNK // 2] + pair[CHUNK // 2 :]
+        top = folded.astype(BF16).astype(F32)
+        return jnp.concatenate([top, folded - top], axis=0)
+
+    tail[...] = as_pieces(pair_att).astype(BF16)
+
+    def att_to_first(k):
+        return remote(tail, att_landed.at[k], att_send.at[0], att_recv.at[k], core, 0)
+
+    @pl.when(me != 0)
+    def _():
+        att_to_first(me).start()
 
     def collect(k, total):
-        to_owner(k).wait_recv()
+        from_owner(k).wait_recv()
         return total + landed[k].astype(F32)
 
     total = lax.fori_loop(1, owners, collect, merged[me].astype(F32))
 
-    chunk[...] = total[share : share + CHUNK].astype(BF16)
+    chunk[...] = total[share:].astype(BF16)
 
     def spread(k):
         e_panel, e_rep = other(k)
         return remote(chunk, chunks.at[index], chunk_send.at[k], chunk_recv.at[k], e_panel, e_rep)
 
     def rows_to(k):
-        part = grad_src_ref.at[pl.ds(pl.multiple_of(rep * share, share), share)]
+        part = rows_ref.at[pl.ds(pl.multiple_of(rep * share, share), share)]
         return remote(part, part, row_send.at[k], row_recv.at[k], panel, lax.rem(rep + k, reps))
 
-    grad_src_ref[pl.ds(pl.multiple_of(rep * share, share), share), :] = total[:share]
+    rows_ref[pl.ds(pl.multiple_of(rep * share, share), share), :] = total[:share]
     each(1, devices, lambda k: spread(k).start())
     each(1, reps, lambda k: rows_to(k).start())
     chunks[index] = chunk[...]
-    att = total[share + CHUNK :]
+
+    def sum_to(k):
+        return remote(
+            att_out_ref, att_out_ref, sum_send.at[k], sum_recv.at[0], k // reps * 2 + core, lax.rem(k, reps)
+        )
+
+    @pl.when(me == 0)
+    def _():
+        def add_att(k, found):
+            att_to_first(k).wait_recv()
+            return found + att_landed[k].astype(F32)
+
+        found = lax.fori_loop(1, owners, add_att, tail[...].astype(F32))
+        att_out_ref[...] = as_pieces(found).astype(BF16)
+        each(1, owners, lambda k: sum_to(k).start())
+        each(1, owners, lambda k: sum_to(k).wait_send())
+
+    @pl.when(me != 0)
+    def _():
+        att_to_first(me).wait_send()
+        sum_to(me).wait_recv()
+
+    each(0, pieces, lambda n: swap(n).wait_send())
+
+    def sent(d):
+        @pl.when(d != me)
+        def _():
+            to_owner(d).wait_send()
+
+    each(0, owners, sent)
+    each(1, devices, lambda k: spread(k).wait())
+    each(1, reps, lambda k: rows_to(k).wait())
+
+
+def unpack_kernel(reps, rows_ref, chunks, att_ref, grad_src_ref, grad_weight_ref, att_src_ref, att_dst_ref):
+    grad_src_ref[...] = rows_ref[...]
+    att = att_ref[...].astype(F32)
     att = att[: CHUNK // 2] + att[CHUNK // 2 :]
     heads, head_dim = att_src_ref.shape
     per = LANES // head_dim
@@ -408,9 +475,6 @@
     ]
     att_src_ref[...] = jnp.concatenate(lines[:heads], axis=0)
     att_dst_ref[...] = jnp.concatenate(lines[heads:], axis=0)
-    each(1, owners, lambda k: to_owner(k).wait_send())
-    each(1, devices, lambda k: spread(k).wait())
-    each(1, reps, lambda k: rows_to(k).wait())
     inputs, width = grad_weight_ref.shape
     half = inputs * width // LANES // CHUNK // 2
     for n in range(2 * half):
@@ -423,37 +487,55 @@
 def reduce(part, part_att, inputs, width, heads, rows):
     owners, lines = part.shape[1:3]
     reps = lax.axis_size("rep")
+    pieces = 4
     vmem = pl.BlockSpec(memory_space=pltpu.VMEM)
     dma = pltpu.SemaphoreType.DMA
+    packed = pl.pallas_call(
+        reduce_kernel,
+        out_shape=(
+            jax.ShapeDtypeStruct((rows, inputs), F32),
+            jax.ShapeDtypeStruct((2 * owners, CHUNK, LANES), BF16),
+            jax.ShapeDtypeStruct((CHUNK, LANES), BF16),
+        ),
+        in_specs=[vmem] * 2,
+        out_specs=(vmem,) * 3,
+        scratch_shapes=[
+            pltpu.VMEM((owners, lines, LANES), BF16),
+            pltpu.VMEM((CHUNK, LANES), BF16),
+            pltpu.VMEM((owners, lines, LANES), BF16),
+            pltpu.VMEM((owners, lines, LANES), BF16),
+            pltpu.VMEM((CHUNK, LANES), BF16),
+            pltpu.VMEM((CHUNK, LANES), BF16),
+            pltpu.VMEM((owners, CHUNK, LANES), BF16),
+            dma((2,)),
+            dma((pieces,)),
+            dma((pieces,)),
+            dma((owners,)),
+            dma((owners,)),
+            dma((reps,)),
+            dma((reps,)),
+            dma((2 * owners,)),
+            dma((2 * owners,)),
+            dma((1,)),
+            dma((owners,)),
+            dma((owners,)),
+            dma((1,)),
+        ],
+        compiler_params=pltpu.CompilerParams(
+            collective_id=1, has_side_effects=True, vmem_limit_bytes=32 * 1024 * 1024
+        ),
+    )(part, part_att)
     return pl.pallas_call(
-        reduce_kernel,
+        functools.partial(unpack_kernel, reps),
         out_shape=(
             jax.ShapeDtypeStruct((rows, inputs), F32),
             jax.ShapeDtypeStruct((inputs, width), F32),
             jax.ShapeDtypeStruct((heads, width // heads), F32),
             jax.ShapeDtypeStruct((heads, width // heads), F32),
         ),
-        in_specs=[vmem] * 2,
+        in_specs=[vmem] * 3,
         out_specs=(vmem,) * 4,
-        scratch_shapes=[
-            pltpu.VMEM((owners, lines, LANES), BF16),
-            pltpu.VMEM((CHUNK, LANES), BF16),
-            pltpu.VMEM((owners, lines + CHUNK, LANES), BF16),
-            pltpu.VMEM((owners, lines + CHUNK, LANES), BF16),
-            pltpu.VMEM((2 * owners, CHUNK, LANES), BF16),
-            pltpu.VMEM((CHUNK, LANES), BF16),
-            dma((4,)),
-            dma((owners,)),
-            dma((owners,)),
-            dma((reps,)),
-            dma((reps,)),
-            dma((2 * owners,)),
-            dma((2 * owners,)),
-        ],
-        compiler_params=pltpu.CompilerParams(
-            collective_id=1, has_side_effects=True, vmem_limit_bytes=62 * 1024 * 1024
-        ),
-    )(part, part_att)
+    )(*packed)
 
 
 def layer(x_all, x_dst, weight, att_src, att_dst, grad_out, rows, cols, masks, counts):

time: 69.2 us -> 67.7 us (0.978); the launches traced: 69.7 us -> 67.4 us
  Pallas kernels: 63.9 us -> 62.5 us
  local copies, waits for them, and re-layouts: 4.42 us -> 3.62 us
    pallas_call x1, Pallas kernels: 35.4 us -> 32.3 us  [reduce(): pl.pallas_call(reduce_kernel, out_shape=(jax.ShapeDtypeStruct((rows, inpu...]
    pallas_call x0 -> x1, Pallas kernels: none -> 1.66 us  [reduce(): pl.pallas_call(functools.partial(unpack_kernel, reps), out_shape=(jax.Sha...]
    unnamed x8 -> x10, local copies, waits for them, and re-layouts: 4.42 us -> 3.62 us
where the time goes in v1:
time: 67.7 us; the launch traced here: 67.4 us
  Pallas kernels  62.5 us (92%)
  local copies, waits for them, and re-layouts  3.62 us (5%)
  between operations  1.31 us (2%)
    pallas_call x1, Pallas kernels, reduce(): pl.pallas_call(reduce_kernel, out_shape=(jax.ShapeDtypeStruct((rows, inpu...  32.3 us
    pallas_call x1, Pallas kernels, layer(): pl.pallas_call(layer_kernel, out_shape=(jax.ShapeDtypeStruct((dest, input...  14.6 us
    pallas_call x1, Pallas kernels, gather(): pl.pallas_call(gather_kernel, out_shape=jax.ShapeDtypeStruct((panels,) +...  13.9 us
    unnamed x10, local copies, waits for them, and re-layouts  3.62 us
    pallas_call x1, Pallas kernels, reduce(): pl.pallas_call(functools.partial(unpack_kernel, reps), out_shape=(jax.Sha...  1.66 us

profile of v1, /device:TPU:0, one launch (start us, length us, event | category | flops | bytes accessed | tf_op | source)
XLA Modules:
  0.0 67.4 jit_solution(1947445687852249921)
XLA Ops:
  1.3 13.9 %shard_map.137 = bf16[16,128,128]{2,1,0:T(8,128)(2,1)} custom-call(bf16[128,128]{1,0:T(8,128)(2,1)} %x_ref.1), custom_call_target="tpu_custom_call" | custom-call | tf_op jit(solution)/shard_map/pallas_call | solution.py:318
  15.2 14.6 %shard_map.138 = (f32[512,128]{1,0:T(8,128)}, bf16[2,16,80,128]{3,2,1,0:T(8,128)(2,1)}, bf16[16,128]{1,0:T(8,128)(2,1)}) custom-call(s32[16]{0:T(128)} %rows_ref.1, s32[16]{0:T(128)} %cols_ref.1, s32[1]{0:T(128)S(6)} %copy.15.count_ref, bf16[2048,128]{1,0:T(8,128)(2,1)} %bitcast.1, bf16[512,128]{1,0:T(8,128)(2,1)} %x_dst_ref.1, bf16[128,512]{1,0:T(8,128)(2,1)} %weight_ref.1, ...), custom_call_target="tpu_custom_call" | custom-call | tf_op jit(solution)/shard_map/pallas_call | solution.py:551
  29.8 0.0 copy-start.3
  29.8 0.7 %copy-done.3 = bf16[16,128]{1,0:T(8,128)(2,1)S(1)} copy-done((bf16[16,128]{1,0:T(8,128)(2,1)S(1)}, bf16[16,128]{1,0:T(8,128)(2,1)}, u32[]{:S(2)}) %copy-start.3) | copy-done | bytes 4120
  30.5 0.0 copy-start
  30.5 1.1 %copy-done = bf16[2,16,80,128]{3,2,1,0:T(8,128)(2,1)S(1)} copy-done((bf16[2,16,80,128]{3,2,1,0:T(8,128)(2,1)S(1)}, bf16[2,16,80,128]{3,2,1,0:T(8,128)(2,1)}, u32[]{:S(2)}) %copy-start) | copy-done | bytes 655384
  31.6 32.3 %shard_map.139 = (f32[128,128]{1,0:T(8,128)S(1)}, bf16[32,16,128]{2,1,0:T(8,128)(2,1)S(1)}, bf16[16,128]{1,0:T(8,128)(2,1)S(1)}) custom-call(bf16[2,16,80,128]{3,2,1,0:T(8,128)(2,1)S(1)} %copy-done, bf16[16,128]{1,0:T(8,128)(2,1)S(1)} %copy-done.3), custom_call_target="tpu_custom_call" | custom-call | tf_op jit(solution)/shard_map/pallas_call | solution.py:493
  63.9 0.0 copy-start.1
  63.9 0.6 copy-done.1
  64.5 0.0 copy-start.2
  64.5 0.6 copy-done.2
  65.1 0.0 copy-start.4
  65.1 0.6 copy-done.4
  65.7 1.7 %shard_map.140 = (f32[128,128]{1,0:T(8,128)}, f32[128,512]{1,0:T(8,128)}, f32[8,64]{1,0:T(8,128)}, f32[8,64]{1,0:T(8,128)}) custom-call(f32[128,128]{1,0:T(8,128)} %copy-done.2, bf16[32,16,128]{2,1,0:T(8,128)(2,1)} %copy-done.1, bf16[16,128]{1,0:T(8,128)(2,1)} %copy-done.4), custom_call_target="tpu_custom_call" | custom-call | tf_op jit(solution)/shard_map/pallas_call | solution.py:528
Async XLA Ops:
  29.8 0.7 %copy-start.3 = (bf16[16,128]{1,0:T(8,128)(2,1)S(1)}, bf16[16,128]{1,0:T(8,128)(2,1)}, u32[]{:S(2)}) copy-start(bf16[16,128]{1,0:T(8,128)(2,1)} %get-tuple-element.16.att_ref) | copy-start | bytes 12292
  30.5 1.1 %copy-start = (bf16[2,16,80,128]{3,2,1,0:T(8,128)(2,1)S(1)}, bf16[2,16,80,128]{3,2,1,0:T(8,128)(2,1)}, u32[]{:S(2)}) copy-start(bf16[2,16,80,128]{3,2,1,0:T(8,128)(2,1)} %get-tuple-element.15.part_ref) | copy-start | bytes 1966084
  63.9 0.7 copy-start.1
  64.5 0.6 copy-start.2
  65.1 0.6 copy-start.4

commit v2 on v1

--- a/solution.py
+++ b/solution.py
@@ -44,10 +44,11 @@
 
 def layer_kernel(
     rows_ref, cols_ref, count_ref, x_all_ref, x_dst_ref, weight_ref, att_src_ref, att_dst_ref,
-    grad_ref, masks_ref,
+    grad_hbm, masks_hbm,
     grad_dst_ref, part_ref, part_att_ref,
     proj_src, proj_turned, proj_dst, cotan_turned, score_src, score_wide, inv_wide, weights, slopes,
     numer, denom, centre, grad_source, grad_score_src, grad_score_dst, source,
+    grad_ref, masks_ref, load_sems,
 ):
     heads, head_dim = att_src_ref.shape
     width = weight_ref.shape[1]
@@ -59,6 +60,11 @@
     owners, share = part_ref.shape[1], part_ref.shape[2] - CHUNK
     reps = x_all_ref.shape[0] // source_blocks // share
     inputs = weight_ref.shape[0]
+
+    load_grad = pltpu.make_async_copy(grad_hbm, grad_ref, load_sems.at[0])
+    load_masks = pltpu.make_async_copy(masks_hbm, masks_ref, load_sems.at[1])
+    load_grad.start()
+    load_masks.start()
 
     lane_head = iota((heads, width), 1) // head_dim
     own = lane_head == iota((heads, width), 0)
@@ -97,6 +103,7 @@
     pre_self = score_d + (shift[3] + shift[4] + shift[5])
     for h in range(heads):
         score_wide[h] = jnp.broadcast_to(score_d[:, h : h + 1], (dest, LANES))
+    load_grad.wait()
     for d in range(dest // blk):
         cotan_turned[d] = grad_ref[d * blk : (d + 1) * blk, :].T
 
@@ -145,6 +152,7 @@
             denom[r, :] += got[:, LANES:]
         return carry
 
+    load_masks.wait()
     lax.fori_loop(0, count, forward, 0)
 
     lanes = iota((dest, LANES), 1)
@@ -327,8 +335,8 @@
 
 
 def reduce_kernel(
-    part_ref, att_ref, rows_ref, chunks, att_out_ref,
-    mate_part, mate_att, merged, landed, chunk, tail, att_landed, mate_sems, swap_send, swap_recv,
+    part_hbm, att_hbm, rows_ref, chunks, att_out_ref,
+    part_ref, att_ref, load_sems, mate_part, mate_att, merged, landed, chunk, tail, att_landed, mate_sems, swap_send, swap_recv,
     send, recv, row_send, row_recv, chunk_send, chunk_recv, att_send, att_recv, sum_send, sum_recv,
 ):
     plane, core, rep, planes, reps = place()
@@ -339,6 +347,10 @@
     panel = plane * 2 + core
     mate = plane * 2 + 1 - core
     index = panel * reps + rep
+    load_part = pltpu.make_async_copy(part_hbm.at[core], part_ref, load_sems.at[0])
+    load_att = pltpu.make_async_copy(att_hbm, att_ref, load_sems.at[1])
+    load_part.start()
+    load_att.start()
     barrier = pltpu.get_barrier_semaphore()
 
     def other(k):
@@ -361,10 +373,10 @@
         n = piece_at(n)
         piece = pl.ds(n * span, span)
         return remote(
-            part_ref.at[1 - core, piece], mate_part.at[piece], swap_send.at[n], swap_recv.at[n], mate, rep
+            part_hbm.at[1 - core, piece], mate_part.at[piece], swap_send.at[n], swap_recv.at[n], mate, rep
         )
 
-    swap_att = remote(att_ref, mate_att, mate_sems.at[0], mate_sems.at[1], mate, rep)
+    swap_att = remote(att_hbm, mate_att, mate_sems.at[0], mate_sems.at[1], mate, rep)
     each(0, pieces, lambda n: swap(n).start())
     swap_att.start()
 
@@ -382,7 +394,7 @@
 
         def merge_send(j):
             d = piece_at(n) * span + lax.rem(me + j, span)
-            summed = part_ref[core, d].astype(F32) + mate_part[d].astype(F32)
+            summed = part_ref[d].astype(F32) + mate_part[d].astype(F32)
             merged[d] = summed.astype(BF16)
 
             @pl.when(d != me)
@@ -391,9 +403,11 @@
 
         each(0, span, merge_send)
 
+    load_part.wait()
     each(0, pieces, merge_piece)
 
     swap_att.wait()
+    load_att.wait()
     pair_att = att_ref[...].astype(F32) + mate_att[...].astype(F32)
 
     def as_pieces(pair):
@@ -497,9 +511,12 @@
             jax.ShapeDtypeStruct((2 * owners, CHUNK, LANES), BF16),
             jax.ShapeDtypeStruct((CHUNK, LANES), BF16),
         ),
-        in_specs=[vmem] * 2,
+        in_specs=[pl.BlockSpec(memory_space=pl.ANY)] * 2,
         out_specs=(vmem,) * 3,
         scratch_shapes=[
+            pltpu.VMEM((owners, lines, LANES), BF16),
+            pltpu.VMEM((CHUNK, LANES), BF16),
+            dma((2,)),
             pltpu.VMEM((owners, lines, LANES), BF16),
             pltpu.VMEM((CHUNK, LANES), BF16),
             pltpu.VMEM((owners, lines, LANES), BF16),
@@ -522,7 +539,7 @@
             dma((1,)),
         ],
         compiler_params=pltpu.CompilerParams(
-            collective_id=1, has_side_effects=True, vmem_limit_bytes=32 * 1024 * 1024
+            collective_id=1, has_side_effects=True, vmem_limit_bytes=62 * 1024 * 1024
         ),
     )(part, part_att)
     return pl.pallas_call(
@@ -535,6 +552,7 @@
         ),
         in_specs=[vmem] * 3,
         out_specs=(vmem,) * 4,
+        compiler_params=pltpu.CompilerParams(vmem_limit_bytes=62 * 1024 * 1024),
     )(*packed)
 
 
@@ -555,7 +573,7 @@
             jax.ShapeDtypeStruct((2, owners, blk // reps + CHUNK, LANES), BF16),
             jax.ShapeDtypeStruct((CHUNK, LANES), BF16),
         ),
-        in_specs=[smem] * 3 + [vmem] * 7,
+        in_specs=[smem] * 3 + [vmem] * 5 + [pl.BlockSpec(memory_space=pl.ANY)] * 2,
         out_specs=(vmem,) * 3,
         scratch_shapes=[
             pltpu.VMEM((sources, width), BF16),
@@ -574,6 +592,9 @@
             pltpu.VMEM((blocks, heads, blk), F32),
             pltpu.VMEM((heads, dest, LANES), F32),
             pltpu.VMEM((width, sources), BF16),
+            pltpu.VMEM(grad_out.shape, grad_out.dtype),
+            pltpu.VMEM(masks.shape, masks.dtype),
+            pltpu.SemaphoreType.DMA((2,)),
         ],
         compiler_params=pltpu.CompilerParams(vmem_limit_bytes=62 * 1024 * 1024),
     )(rows, cols, counts, x_all, x_dst, weight, att_src, att_dst, grad_out, masks)

time: 67.7 us -> 64.1 us (0.947)
  local copies, waits for them, and re-layouts: 3.62 us -> 0 us
    pallas_call x1, Pallas kernels: 32.3 us -> 23.1 us  [reduce(): pl.pallas_call(reduce_kernel, out_shape=(jax.ShapeDtypeStruct((rows, inpu...]
    pallas_call x1, Pallas kernels: 14.6 us -> 23.6 us  [layer(): pl.pallas_call(layer_kernel, out_shape=(jax.ShapeDtypeStruct((dest, input...]
    unnamed x10 -> x0, local copies, waits for them, and re-layouts: 3.62 us -> none
where the time goes in v2:
time: 64.1 us; the launch traced here: 63.5 us
  Pallas kernels  62.2 us (97%)
  between operations  1.3 us (2%)
    pallas_call x1, Pallas kernels, layer(): pl.pallas_call(layer_kernel, out_shape=(jax.ShapeDtypeStruct((dest, input...  23.6 us
    pallas_call x1, Pallas kernels, reduce(): pl.pallas_call(reduce_kernel, out_shape=(jax.ShapeDtypeStruct((rows, inpu...  23.1 us
    pallas_call x1, Pallas kernels, gather(): pl.pallas_call(gather_kernel, out_shape=jax.ShapeDtypeStruct((panels,) +...  13.9 us
    pallas_call x1, Pallas kernels, reduce(): pl.pallas_call(functools.partial(unpack_kernel, reps), out_shape=(jax.Sha...  1.66 us

profile of v2, /device:TPU:0, one launch (start us, length us, event | category | flops | bytes accessed | tf_op | source)
XLA Modules:
  0.0 63.5 jit_solution(15108995369813659888)
XLA Ops:
  1.3 13.9 %shard_map.137 = bf16[16,128,128]{2,1,0:T(8,128)(2,1)} custom-call(bf16[128,128]{1,0:T(8,128)(2,1)} %x_ref.1), custom_call_target="tpu_custom_call" | custom-call | tf_op jit(solution)/shard_map/pallas_call | solution.py:326
  15.1 23.6 %shard_map.138 = (f32[512,128]{1,0:T(8,128)}, bf16[2,16,80,128]{3,2,1,0:T(8,128)(2,1)}, bf16[16,128]{1,0:T(8,128)(2,1)}) custom-call(s32[16]{0:T(128)} %rows_ref.1, s32[16]{0:T(128)} %cols_ref.1, s32[1]{0:T(128)S(6)} %copy.15.count_ref, bf16[2048,128]{1,0:T(8,128)(2,1)} %bitcast.1, bf16[512,128]{1,0:T(8,128)(2,1)} %x_dst_ref.1, bf16[128,512]{1,0:T(8,128)(2,1)} %weight_ref.1, ...), custom_call_target="tpu_custom_call" | custom-call | tf_op jit(solution)/shard_map/pallas_call | solution.py:569
  38.7 23.1 %shard_map.139 = (f32[128,128]{1,0:T(8,128)}, bf16[32,16,128]{2,1,0:T(8,128)(2,1)}, bf16[16,128]{1,0:T(8,128)(2,1)}) custom-call(bf16[2,16,80,128]{3,2,1,0:T(8,128)(2,1)} %get-tuple-element.15.part_hbm, bf16[16,128]{1,0:T(8,128)(2,1)} %get-tuple-element.16.att_hbm), custom_call_target="tpu_custom_call" | custom-call | tf_op jit(solution)/shard_map/pallas_call | solution.py:507
  61.8 1.7 %shard_map.140 = (f32[128,128]{1,0:T(8,128)}, f32[128,512]{1,0:T(8,128)}, f32[8,64]{1,0:T(8,128)}, f32[8,64]{1,0:T(8,128)}) custom-call(f32[128,128]{1,0:T(8,128)} %get-tuple-element.17.rows_ref, bf16[32,16,128]{2,1,0:T(8,128)(2,1)} %get-tuple-element.18.chunks, bf16[16,128]{1,0:T(8,128)(2,1)} %get-tuple-element.19.att_ref), custom_call_target="tpu_custom_call" | custom-call | tf_op jit(solution)/shard_map/pallas_call | solution.py:545
